TPU v7x, 32 devices: a whole 2x2x4 slice. The times are simulated.
32 devices in a mesh: groups: 2 (over x), query: 16 (over z, y, core).
Axes of the slice: x: 2, y: 2, z: 4, core: 2. Of those that a mesh axis runs over, the one named last changes fastest.
Arguments:
- tokens: bfloat16 [384, 4096], P(('groups', 'query')), parts along dimension 0, may hold values from -6 to 6
- grad_out: bfloat16 [384, 4096], P(('groups', 'query')), parts along dimension 0, may hold values from -6 to 6
- gate_weight: bfloat16 [4096, 14336], P(None, 'query'), may hold values from -0.09375 to 0.09375
- up_weight: bfloat16 [4096, 14336], P(None, 'query'), may hold values from -0.09375 to 0.09375
- query_left: bfloat16 [16, 4096, 32], P('query'), may hold values from -0.09375 to 0.09375
- query_right: bfloat16 [16, 14336, 32], P('query'), may hold values from -0.09375 to 0.09375
Outputs:
- scores: float32 [384, 16], P(('groups', 'query')), parts along dimension 0
There are 2 independent parts, one for each index of `groups`. A program takes and returns all parts, laid end to end along the dimension named above; an argument that names none is the same for every part. Nothing has to cross between parts.
All inputs are finite; a program needn't handle non-finite values.
Results may differ from a plain program's by a relative error of at most 0.0003.
Values may be sent and summed in bfloat16 or wider, within the bound.
No kernel may reach another device: no remote copies, remote signals or barrier semaphores. Data moves between devices by JAX's collectives and lax.ppermute only.
A program may use at most 128 MiB of HBM per device.

v0:
```python
import jax
import jax.numpy as jnp
from jax import lax
from jax.sharding import PartitionSpec as P


def body(tokens, grad_out, gate_weight, up_weight, query_left, query_right):
    whole = lax.all_gather(tokens, "query", axis=0, tiled=True)
    right_cols = lax.all_to_all(query_right, "query", split_axis=1, concat_axis=0, tiled=True)
    right_wide = right_cols.astype(jnp.float32)
    num_queries = right_cols.shape[0]
    rank_size = right_cols.shape[2]
    tok_rows = tokens.shape[0]
    gate = jnp.dot(whole, gate_weight, preferred_element_type=jnp.float32)
    up = jnp.dot(whole, up_weight, preferred_element_type=jnp.float32)
    hidden = jax.nn.silu(gate) * up
    term = jnp.einsum("tf,qfr->tqr", hidden, right_wide, precision=lax.Precision.HIGHEST)
    proj_right = lax.psum_scatter(
        term.reshape(tok_rows * lax.axis_size("query"), num_queries * rank_size),
        "query",
        scatter_dimension=0,
        tiled=True,
    )
    proj_right = proj_right.reshape(tok_rows, num_queries, rank_size)
    left = jnp.einsum(
        "td,kdr->tkr",
        grad_out,
        lax.all_gather(query_left, "query", axis=0, tiled=True),
        preferred_element_type=jnp.float32,
    )
    return jnp.sum(left * proj_right, axis=2)


def solution(mesh):
    return jax.shard_map(
        body,
        mesh=mesh,
        in_specs=(
            P(("groups", "query"), None),
            P(("groups", "query"), None),
            P(None, "query"),
            P(None, "query"),
            P("query", None, None),
            P("query", None, None),
        ),
        out_specs=P(("groups", "query"), None),
        check_vma=False,
    )
```

profile of v0, /device:TPU:17, one launch (start us, length us, event | category | flops | bytes accessed | tf_op | source)
XLA Modules:
  0.0 230.3 jit_solution(11249629762622206637)
XLA Ops:
  6.5 0.0 copy-start
  6.5 0.0 all-gather.6.cloned.1.call-start
  6.5 0.7 all-gather.6.cloned.1.call-update
  7.3 0.0 all-gather.4.cloned.1.call-start
  7.3 0.7 all-gather.4.cloned.1.call-update
  8.0 14.3 %copy.10 = bf16[1,14336,32]{2,0,1:T(2,128)(2,1)} copy(bf16[1,14336,32]{1,2,0:T(8,128)(2,1)} %param.11) | data formatting | bytes 1835008 | tf_op args[5]
  22.3 0.5 broadcast.2
  22.8 79.8 %reduce = bf16[14336,32]{1,0:T(8,128)(2,1)} reduce(bf16[14336,1,32]{2,1,0:T(2,128)(2,1)} %bitcast.26, bf16[]{:T(256)} %broadcast.2), dimensions={1}, to_apply=%bitcast.15.reduce_sub_computation | reduce | bytes 1835010
  102.6 5.0 %reshape.13 = bf16[16,2,14336]{2,1,0:T(2,128)(2,1)S(1)} reshape(bf16[14336,32]{1,0:T(8,128)(2,1)} %reduce) | data formatting | bytes 1835008
  107.5 27.9 %all_to_all.12 = bf16[16,2,14336]{2,1,0:T(2,128)(2,1)S(1)} all-to-all(bf16[16,2,14336]{2,1,0:T(2,128)(2,1)S(1)} %reshape.13), channel_id=1, replica_groups=mesh['groups'=2,'query'=16] {'query'}, dimensions={0} | all-to-all | bytes 1835008 | tf_op jit(solution)/shard_map/all_to_all | solution.py:9
  135.4 8.4 %reshape.14 = bf16[14336,1,32]{2,1,0:T(2,128)(2,1)} reshape(bf16[16,2,14336]{2,1,0:T(2,128)(2,1)S(1)} %all_to_all.12) | data formatting | bytes 1835008
  143.8 13.7 %copy.11 = bf16[1,14336,32]{1,2,0:T(8,128)(2,1)S(1)} copy(bf16[1,14336,32]{2,0,1:T(2,128)(2,1)} %bitcast.27) | data formatting | bytes 1835008 | tf_op jit(solution)/shard_map/all_to_all | solution.py:9
  157.5 0.1 copy.15
  157.6 0.2 copy.12
  157.8 0.0 all-gather.6.cloned.1.call-done
  157.8 2.5 %reshape.10 = bf16[192,4096]{1,0:T(8,128)(2,1)S(1)} reshape(bf16[16,12,4096]{2,1,0:T(8,128)(2,1)} %all-gather.6.cloned.1.call-done) | data formatting | bytes 3145728
  160.3 4.9 %fusion.4 = f32[192,896]{1,0:T(8,128)S(1)} fusion(bf16[192,4096]{1,0:T(8,128)(2,1)S(1)} %reshape.10, bf16[4096,896]{1,0:T(8,128)(2,1)} %param.8), kind=kOutput, calls=%fused_computation.6 | convolution fusion | flops 1409286144 | bytes 9601024 | tf_op jit(solution)/shard_map/dot_general | solution.py:14
  165.2 0.0 copy-start.1
  165.2 4.9 %convolution_multiply_fusion = f32[192,896]{1,0:T(8,128)S(1)} fusion(bf16[192,4096]{1,0:T(8,128)(2,1)S(1)} %reshape.10, bf16[4096,896]{1,0:T(8,128)(2,1)} %param.9, f32[192,896]{1,0:T(8,128)S(1)} %fusion.4), kind=kOutput, calls=%fused_computation | convolution fusion | flops 1410146304 | bytes 10289152 | tf_op jit(solution)/shard_map/dot_general | solution.py:15
  170.1 1.1 fusion.5
  171.2 25.9 %fusion = f32[16,512]{1,0:T(8,128)S(1)} fusion(f32[192,512]{1,0:T(8,128)S(1)} %fusion.5), kind=kCustom, calls=%all-reduce-scatter | all-reduce-scatter fusion | flops 131073 | bytes 426496
  197.1 2.8 %collective-permute-start = (f32[16,512]{1,0:T(8,128)S(1)}, f32[16,512]{1,0:T(8,128)S(1)}, u32[]{:S(2)}, u32[]{:S(2)}) collective-permute-start(f32[16,512]{1,0:T(8,128)S(1)} %fusion), channel_id=1, source_target_pairs={{0,1},{1,2},{2,3},{3,4},{4,5},{5,6},{6,7},{7,8},{8,9},{9,10},{10,1... | collective-permute-start | bytes 98312
  199.9 5.0 %collective-permute-start.1 = (f32[16,512]{1,0:T(8,128)S(1)}, f32[16,512]{1,0:T(8,128)S(1)}, u32[]{:S(2)}, u32[]{:S(2)}) collective-permute-start(f32[16,512]{1,0:T(8,128)S(1)} %fusion), channel_id=1, source_target_pairs={{0,2},{1,3},{2,4},{3,5},{4,6},{5,7},{6,8},{7,9},{8,10},{9,11},{10,... | collective-permute-start | bytes 98312
  204.8 7.5 %collective-permute-start.2 = (f32[16,512]{1,0:T(8,128)S(1)}, f32[16,512]{1,0:T(8,128)S(1)}, u32[]{:S(2)}, u32[]{:S(2)}) collective-permute-start(f32[16,512]{1,0:T(8,128)S(1)} %fusion), channel_id=1, source_target_pairs={{0,3},{1,4},{2,5},{3,6},{4,7},{5,8},{6,9},{7,10},{8,11},{9,12},{10... | collective-permute-start | bytes 98312
  212.3 1.9 collective-permute-start.3
  214.2 0.0 copy-done.1
  214.3 0.6 dynamic-slice.4
  215.5 1.5 collective-permute-done.3
  217.0 0.0 collective-permute-done
  217.0 0.0 collective-permute-done.1
  217.0 0.0 collective-permute-done.2
  217.0 0.5 concatenate
  217.5 0.1 reshape.8
  217.6 0.0 all-gather.4.cloned.1.call-done
  217.6 0.0 copy-done
  217.6 5.1 %fusion.3 = f32[12,16]{0,1:T(8,128)S(1)} fusion(f32[12,16,32]{2,1,0:T(8,128)S(1)} %reshape.8, bf16[16,4096,32]{1,2,0:T(8,128)(2,1)} %all-gather.4.cloned.1.call-done, bf16[12,4096]{1,0:T(8,128)(2,1)S(1)} %copy-done), kind=kOutput, calls=%fused_computation.4 | convolution fusion | flops 50343744 | bytes 4317952 | tf_op jit(solution)/shard_map/td,kdr->tkr/dot_general | solution.py:25
  222.7 0.7 copy.14
  (2 shorter events, 0.0 us)
Async XLA Ops:
  6.5 211.1 %copy-start = (bf16[12,4096]{1,0:T(8,128)(2,1)S(1)}, bf16[12,4096]{1,0:T(8,128)(2,1)}, u32[]{:S(2)}) copy-start(bf16[12,4096]{1,0:T(8,128)(2,1)} %param.7) | copy-start | bytes 294916
  6.5 151.2 %all-gather.6.cloned.1.call-start = ((), (), s32[]{:S(2)}) async-start(), calls=%async_computation.2 | async-start | bytes 2228224 | tf_op jit(solution)/shard_map/all_gather | solution.py:8
  7.3 210.4 %all-gather.4.cloned.1.call-start = ((), (), s32[]{:S(2)}) async-start(), calls=%async_computation.1 | async-start | bytes 4456448 | tf_op jit(solution)/shard_map/all_gather | solution.py:28
  165.2 49.1 %copy-start.1 = (u32[32]{0:T(128)S(1)}, u32[32]{0:T(128)}, u32[]{:S(2)}) copy-start(u32[32]{0:T(128)} %constant.11) | copy-start | bytes 388
  197.1 19.9 %collective-permute-start = (f32[16,512]{1,0:T(8,128)S(1)}, f32[16,512]{1,0:T(8,128)S(1)}, u32[]{:S(2)}, u32[]{:S(2)}) collective-permute-start(f32[16,512]{1,0:T(8,128)S(1)} %fusion), channel_id=1, source_target_pairs={{0,1},{1,2},{2,3},{3,4},{4,5},{5,6},{6,7},{7,8},{8,9},{9,10},{10,1... | collective-permute-start | bytes 98312
  199.9 17.1 %collective-permute-start.1 = (f32[16,512]{1,0:T(8,128)S(1)}, f32[16,512]{1,0:T(8,128)S(1)}, u32[]{:S(2)}, u32[]{:S(2)}) collective-permute-start(f32[16,512]{1,0:T(8,128)S(1)} %fusion), channel_id=1, source_target_pairs={{0,2},{1,3},{2,4},{3,5},{4,6},{5,7},{6,8},{7,9},{8,10},{9,11},{10,... | collective-permute-start | bytes 98312
  204.8 12.1 %collective-permute-start.2 = (f32[16,512]{1,0:T(8,128)S(1)}, f32[16,512]{1,0:T(8,128)S(1)}, u32[]{:S(2)}, u32[]{:S(2)}) collective-permute-start(f32[16,512]{1,0:T(8,128)S(1)} %fusion), channel_id=1, source_target_pairs={{0,3},{1,4},{2,5},{3,6},{4,7},{5,8},{6,9},{7,10},{8,11},{9,12},{10... | collective-permute-start | bytes 98312
  212.3 4.7 %collective-permute-start.3 = (f32[12,512]{1,0:T(8,128)S(1)}, f32[12,512]{1,0:T(8,128)S(1)}, u32[]{:S(2)}, u32[]{:S(2)}) collective-permute-start(f32[12,512]{1,0:T(8,128)S(1)} %slice), channel_id=1, source_target_pairs={{0,4},{1,5},{2,6},{3,7},{4,8},{5,9},{6,10},{7,11},{8,12},{9,13},{1... | collective-permute-start | bytes 73736
Sparse Core Ops, SparseCore 0:
  9.5 41.0 all-gather.5
  52.8 50.6 all-gather.3
where the time goes:
time: 232 us; the launch traced here: 230 us
  other arithmetic  79.8 us (34%)
  blocking collectives  53.8 us (23%)
  local copies, waits for them, and re-layouts  46.4 us (20%)
  starting transfers between devices  17.2 us (7%)
  matrix products  16 us (7%)
  between operations  14.2 us (6%)
  waiting for transfers between devices  2.94 us (1%)
    unnamed x1, other arithmetic  79.8 us
    unnamed x14, local copies, waits for them, and re-layouts  31.8 us
    all_to_all x1, blocking collectives, body(): lax.all_to_all(query_right, 'query', split_axis=1, concat_axis=0, tiled=T...  27.9 us
    unnamed x1, blocking collectives  25.9 us
    unnamed x4, starting transfers between devices  17.1 us
    all_to_all x1, local copies, waits for them, and re-layouts, body(): lax.all_to_all(query_right, 'query', split_axis=1, concat_axis=0, tiled=T...  13.7 us
    dot_general x1, matrix products, body(): jnp.einsum('td,kdr->tkr', grad_out, lax.all_gather(query_left, 'query', a...  5.07 us
    dot_general x1, matrix products, body(): up = jnp.dot(whole, up_weight, preferred_element_type=jnp.float32)  4.93 us
  transfers between devices with their start and end apart: 6, of which 1 were waited for; matrix products, arithmetic and copies ran while one was open for 70% of the time, Pallas kernels for 0%

commit v1 on v0

--- a/solution.py
+++ b/solution.py
@@ -4,9 +4,25 @@
 from jax.sharding import PartitionSpec as P
 
 
+def pairwise_exchange(x, axis, split, join):
+    ways, here = (lax.axis_size(axis), lax.axis_index(axis))
+    width = x.shape[split] // ways
+    shape = list(x.shape)
+    shape[split] = width
+    height = shape[join]
+    shape[join] = height * ways
+    full = jnp.zeros(shape, x.dtype)
+    for mask in range(ways):
+        part = lax.dynamic_slice_in_dim(x, (here ^ mask) * width, width, axis=split)
+        if mask:
+            part = lax.ppermute(part, axis, [(d, d ^ mask) for d in range(ways)])
+        full = lax.dynamic_update_slice_in_dim(full, part, (here ^ mask) * height, axis=join)
+    return full
+
+
 def body(tokens, grad_out, gate_weight, up_weight, query_left, query_right):
     whole = lax.all_gather(tokens, "query", axis=0, tiled=True)
-    right_cols = lax.all_to_all(query_right, "query", split_axis=1, concat_axis=0, tiled=True)
+    right_cols = pairwise_exchange(query_right, "query", 1, 0)
     right_wide = right_cols.astype(jnp.float32)
     num_queries = right_cols.shape[0]
     rank_size = right_cols.shape[2]

time: 232 us -> 138 us (0.59)
  other arithmetic: 79.8 us -> 0 us
  local copies, waits for them, and re-layouts: 46.4 us -> 5.98 us
  waiting for transfers between devices: 2.94 us -> 28.7 us
  starting transfers between devices: 17.2 us -> 41.8 us
  blocking collectives: 53.8 us -> 29.8 us
    unnamed x1 -> x0, other arithmetic: 79.8 us -> none
    unnamed x14 -> x9, local copies, waits for them, and re-layouts: 31.8 us -> 3.57 us
    all_to_all x1 -> x0, blocking collectives: 27.9 us -> none  [body(): lax.all_to_all(query_right, 'query', split_axis=1, concat_axis=0, tiled=T...]
    ppermute x0 -> x15, starting transfers between devices: none -> 24.1 us  [pairwise_exchange(): part = lax.ppermute(part, axis, [(d, d ^ mask) for d in range(ways)])]
    all_gather x1, waiting for transfers between devices: 0.02 us -> 14.7 us  [body(): whole = lax.all_gather(tokens, 'query', axis=0, tiled=True)]
    all_to_all x1 -> x0, local copies, waits for them, and re-layouts: 13.7 us -> none  [body(): lax.all_to_all(query_right, 'query', split_axis=1, concat_axis=0, tiled=T...]
    ppermute x0 -> x15, waiting for transfers between devices: none -> 11.1 us  [pairwise_exchange(): part = lax.ppermute(part, axis, [(d, d ^ mask) for d in range(ways)])]
    unnamed x1, blocking collectives: 25.9 us -> 29.8 us
  transfers between devices with their start and end apart: 6 -> 21, of which waited for: 1 -> 7; matrix products, arithmetic and copies ran while one was open for 70% -> 34% of each run, Pallas kernels for 0% -> 0%
where the time goes in v1:
time: 138 us; the launch traced here: 137 us
  starting transfers between devices  41.8 us (30%)
  blocking collectives  29.8 us (22%)
  waiting for transfers between devices  28.7 us (21%)
  matrix products  16.1 us (12%)
  between operations  14.4 us (10%)
  local copies, waits for them, and re-layouts  5.98 us (4%)
    unnamed x1, blocking collectives  29.8 us
    ppermute x15, starting transfers between devices, pairwise_exchange(): part = lax.ppermute(part, axis, [(d, d ^ mask) for d in range(ways)])  24.1 us
    unnamed x4, starting transfers between devices  17.7 us
    all_gather x1, waiting for transfers between devices, body(): whole = lax.all_gather(tokens, 'query', axis=0, tiled=True)  14.7 us
    ppermute x15, waiting for transfers between devices, pairwise_exchange(): part = lax.ppermute(part, axis, [(d, d ^ mask) for d in range(ways)])  11.1 us
    dot_general x1, matrix products, body(): jnp.einsum('td,kdr->tkr', grad_out, lax.all_gather(query_left, 'query', a...  5.07 us
    dot_general x1, matrix products, body(): up = jnp.dot(whole, up_weight, preferred_element_type=jnp.float32)  5.03 us
    dot_general x1, matrix products, body(): gate = jnp.dot(whole, gate_weight, preferred_element_type=jnp.float32)  4.93 us
  transfers between devices with their start and end apart: 21, of which 7 were waited for; matrix products, arithmetic and copies ran while one was open for 34% of the time, Pallas kernels for 0%

profile of v1, /device:TPU:17, one launch (start us, length us, event | category | flops | bytes accessed | tf_op | source)
XLA Modules:
  0.0 136.8 jit_solution(2021953732171861589)
XLA Ops:
  6.5 0.7 all-gather.6.cloned.1.call-update
  7.3 0.0 all-gather.4.cloned.1.call-start
  7.3 0.7 all-gather.4.cloned.1.call-update
  8.1 0.1 broadcast_in_dim.3
  8.2 1.4 constant_dynamic-slice_fusion
  9.6 0.7 collective-permute-start
  10.3 1.3 collective-permute-start.1
  11.6 0.5 collective-permute-start.2
  12.0 1.3 collective-permute-start.3
  13.3 0.5 collective-permute-start.4
  13.8 2.3 %collective-permute-start.5 = (bf16[1,896,32]{1,2,0:T(8,128)(2,1)S(1)}, bf16[1,896,32]{1,2,0:T(8,128)(2,1)S(1)}, u32[]{:S(2)}, u32[]{:S(2)}) collective-permute-start(bf16[1,896,32]{1,2,0:T(8,128)(2,1)S(1)} %get-tuple-element.13), channel_id=1, source_target_pairs={{0,6},{1,7},{2,4},{3,5},{4,2},{5,3},{6,0},{7,1},{8,14},{9,15},{10,... | collective-permute-start | bytes 172040 | tf_op jit(solution)/shard_map/ppermute | solution.py:18
  16.1 0.0 collective-permute-done.1
  16.1 1.1 collective-permute-start.6
  17.3 0.1 collective-permute-start.7
  17.4 0.0 collective-permute-done.3
  17.4 2.0 %collective-permute-start.8 = (bf16[1,896,32]{1,2,0:T(8,128)(2,1)S(1)}, bf16[1,896,32]{1,2,0:T(8,128)(2,1)S(1)}, u32[]{:S(2)}, u32[]{:S(2)}) collective-permute-start(bf16[1,896,32]{1,2,0:T(8,128)(2,1)S(1)} %get-tuple-element.10), channel_id=1, source_target_pairs={{0,9},{1,8},{2,11},{3,10},{4,13},{5,12},{6,15},{7,14},{8,1},{9,0},... | collective-permute-start | bytes 172040 | tf_op jit(solution)/shard_map/ppermute | solution.py:18
  19.4 0.0 collective-permute-done.4
  19.4 1.1 collective-permute-start.9
  20.5 0.0 collective-permute-done.5
  20.5 3.3 %collective-permute-start.10 = (bf16[1,896,32]{1,2,0:T(8,128)(2,1)S(1)}, bf16[1,896,32]{1,2,0:T(8,128)(2,1)S(1)}, u32[]{:S(2)}, u32[]{:S(2)}) collective-permute-start(bf16[1,896,32]{1,2,0:T(8,128)(2,1)S(1)} %get-tuple-element.8), channel_id=1, source_target_pairs={{0,11},{1,10},{2,9},{3,8},{4,15},{5,14},{6,13},{7,12},{8,3},{9,2},... | collective-permute-start | bytes 172040 | tf_op jit(solution)/shard_map/ppermute | solution.py:18
  23.8 0.1 collective-permute-start.11
  23.9 5.9 %collective-permute-start.12 = (bf16[1,896,32]{1,2,0:T(8,128)(2,1)S(1)}, bf16[1,896,32]{1,2,0:T(8,128)(2,1)S(1)}, u32[]{:S(2)}, u32[]{:S(2)}) collective-permute-start(bf16[1,896,32]{1,2,0:T(8,128)(2,1)S(1)} %get-tuple-element.6), channel_id=1, source_target_pairs={{0,13},{1,12},{2,15},{3,14},{4,9},{5,8},{6,11},{7,10},{8,5},{9,4},... | collective-permute-start | bytes 172040 | tf_op jit(solution)/shard_map/ppermute | solution.py:18
  29.8 0.0 collective-permute-done.8
  29.9 2.1 %collective-permute-start.13 = (bf16[1,896,32]{1,2,0:T(8,128)(2,1)S(1)}, bf16[1,896,32]{1,2,0:T(8,128)(2,1)S(1)}, u32[]{:S(2)}, u32[]{:S(2)}) collective-permute-start(bf16[1,896,32]{1,2,0:T(8,128)(2,1)S(1)} %get-tuple-element.20), channel_id=1, source_target_pairs={{0,14},{1,15},{2,12},{3,13},{4,10},{5,11},{6,8},{7,9},{8,6},{9,7},... | collective-permute-start | bytes 172040 | tf_op jit(solution)/shard_map/ppermute | solution.py:18
  32.0 1.9 %collective-permute-start.14 = (bf16[1,896,32]{1,2,0:T(8,128)(2,1)S(1)}, bf16[1,896,32]{1,2,0:T(8,128)(2,1)S(1)}, u32[]{:S(2)}, u32[]{:S(2)}) collective-permute-start(bf16[1,896,32]{1,2,0:T(8,128)(2,1)S(1)} %get-tuple-element.5), channel_id=1, source_target_pairs={{0,15},{1,14},{2,13},{3,12},{4,11},{5,10},{6,9},{7,8},{8,7},{9,6},... | collective-permute-start | bytes 172040 | tf_op jit(solution)/shard_map/ppermute | solution.py:18
  33.9 0.4 collective-permute-done.10
  34.3 4.8 %collective-permute-done.11 = bf16[1,896,32]{1,2,0:T(8,128)(2,1)S(1)} collective-permute-done((bf16[1,896,32]{1,2,0:T(8,128)(2,1)S(1)}, bf16[1,896,32]{1,2,0:T(8,128)(2,1)S(1)}, u32[]{:S(2)}, u32[]{:S(2)}) %collective-permute-start.11) | collective-permute-done | bytes 57376 | tf_op jit(solution)/shard_map/ppermute | solution.py:18
  39.1 2.5 %collective-permute-done.12 = bf16[1,896,32]{1,2,0:T(8,128)(2,1)S(1)} collective-permute-done((bf16[1,896,32]{1,2,0:T(8,128)(2,1)S(1)}, bf16[1,896,32]{1,2,0:T(8,128)(2,1)S(1)}, u32[]{:S(2)}, u32[]{:S(2)}) %collective-permute-start.12) | collective-permute-done | bytes 57376 | tf_op jit(solution)/shard_map/ppermute | solution.py:18
  41.6 2.2 %collective-permute-done.13 = bf16[1,896,32]{1,2,0:T(8,128)(2,1)S(1)} collective-permute-done((bf16[1,896,32]{1,2,0:T(8,128)(2,1)S(1)}, bf16[1,896,32]{1,2,0:T(8,128)(2,1)S(1)}, u32[]{:S(2)}, u32[]{:S(2)}) %collective-permute-start.13) | collective-permute-done | bytes 57376 | tf_op jit(solution)/shard_map/ppermute | solution.py:18
  43.8 1.2 collective-permute-done.14
  45.0 14.7 %all-gather.6.cloned.1.call-done = bf16[16,12,4096]{2,1,0:T(8,128)(2,1)} async-done(((bf16[1,12,4096]{2,1,0:T(8,128)(2,1)}), bf16[16,12,4096]{2,1,0:T(8,128)(2,1)}) %all-gather.6.cloned.1.call-update) | async-done | bytes 1572880 | tf_op jit(solution)/shard_map/all_gather | solution.py:24
  59.7 2.5 %reshape.9 = bf16[192,4096]{1,0:T(8,128)(2,1)S(1)} reshape(bf16[16,12,4096]{2,1,0:T(8,128)(2,1)} %all-gather.6.cloned.1.call-done) | data formatting | bytes 3145728
  62.2 4.9 %fusion.4 = f32[192,896]{1,0:T(8,128)S(1)} fusion(bf16[192,4096]{1,0:T(8,128)(2,1)S(1)} %reshape.9, bf16[4096,896]{1,0:T(8,128)(2,1)} %param.8), kind=kOutput, calls=%fused_computation.37 | convolution fusion | flops 1409286144 | bytes 9601024 | tf_op jit(solution)/shard_map/dot_general | solution.py:30
  67.1 0.0 copy-start.1
  67.1 5.0 %convolution_multiply_fusion = f32[192,896]{1,0:T(8,128)S(1)} fusion(bf16[192,4096]{1,0:T(8,128)(2,1)S(1)} %reshape.9, bf16[4096,896]{1,0:T(8,128)(2,1)} %param.9, f32[192,896]{1,0:T(8,128)S(1)} %fusion.4), kind=kOutput, calls=%fused_computation | convolution fusion | flops 1410146304 | bytes 10289152 | tf_op jit(solution)/shard_map/dot_general | solution.py:31
  72.2 1.1 fusion.5
  73.3 29.8 %fusion = f32[16,512]{1,0:T(8,128)S(1)} fusion(f32[192,512]{1,0:T(8,128)S(1)} %fusion.5), kind=kCustom, calls=%all-reduce-scatter | all-reduce-scatter fusion | flops 131073 | bytes 426496
  103.0 4.8 %collective-permute-start.17 = (f32[16,512]{1,0:T(8,128)S(1)}, f32[16,512]{1,0:T(8,128)S(1)}, u32[]{:S(2)}, u32[]{:S(2)}) collective-permute-start(f32[16,512]{1,0:T(8,128)S(1)} %fusion), channel_id=1, source_target_pairs={{0,3},{1,4},{2,5},{3,6},{4,7},{5,8},{6,9},{7,10},{8,11},{9,12},{10... | collective-permute-start | bytes 98312
  107.8 5.1 %collective-permute-start.16 = (f32[16,512]{1,0:T(8,128)S(1)}, f32[16,512]{1,0:T(8,128)S(1)}, u32[]{:S(2)}, u32[]{:S(2)}) collective-permute-start(f32[16,512]{1,0:T(8,128)S(1)} %fusion), channel_id=1, source_target_pairs={{0,2},{1,3},{2,4},{3,5},{4,6},{5,7},{6,8},{7,9},{8,10},{9,11},{10,... | collective-permute-start | bytes 98312
  113.0 5.8 %collective-permute-start.15 = (f32[16,512]{1,0:T(8,128)S(1)}, f32[16,512]{1,0:T(8,128)S(1)}, u32[]{:S(2)}, u32[]{:S(2)}) collective-permute-start(f32[16,512]{1,0:T(8,128)S(1)} %fusion), channel_id=1, source_target_pairs={{0,1},{1,2},{2,3},{3,4},{4,5},{5,6},{6,7},{7,8},{8,9},{9,10},{10,1... | collective-permute-start | bytes 98312
  118.8 1.9 %collective-permute-start.18 = (f32[12,512]{1,0:T(8,128)S(1)}, f32[12,512]{1,0:T(8,128)S(1)}, u32[]{:S(2)}, u32[]{:S(2)}) collective-permute-start(f32[12,512]{1,0:T(8,128)S(1)} %slice), channel_id=1, source_target_pairs={{0,4},{1,5},{2,6},{3,7},{4,8},{5,9},{6,10},{7,11},{8,12},{9,13},{1... | collective-permute-start | bytes 73736
  120.8 0.6 dynamic-slice.4
  122.0 1.5 %collective-permute-done.18 = f32[12,512]{1,0:T(8,128)S(1)} collective-permute-done((f32[12,512]{1,0:T(8,128)S(1)}, f32[12,512]{1,0:T(8,128)S(1)}, u32[]{:S(2)}, u32[]{:S(2)}) %collective-permute-start.18) | collective-permute-done | bytes 24608
  123.5 0.5 concatenate
  124.0 0.1 reshape.7
  124.1 0.0 all-gather.4.cloned.1.call-done
  124.1 5.1 %fusion.3 = f32[12,16]{0,1:T(8,128)S(1)} fusion(f32[12,16,32]{2,1,0:T(8,128)S(1)} %reshape.7, bf16[16,4096,32]{1,2,0:T(8,128)(2,1)} %all-gather.4.cloned.1.call-done, bf16[12,4096]{1,0:T(8,128)(2,1)S(1)} %copy-done), kind=kOutput, calls=%fused_computation.4 | convolution fusion | flops 50343744 | bytes 4317952 | tf_op jit(solution)/shard_map/td,kdr->tkr/dot_general | solution.py:41
  129.2 0.7 copy.11
  (29 shorter events, 0.2 us)
Async XLA Ops:
  6.5 117.6 %copy-start = (bf16[12,4096]{1,0:T(8,128)(2,1)S(1)}, bf16[12,4096]{1,0:T(8,128)(2,1)}, u32[]{:S(2)}) copy-start(bf16[12,4096]{1,0:T(8,128)(2,1)} %param.7) | copy-start | bytes 294916
  6.5 53.2 %all-gather.6.cloned.1.call-start = ((), (), s32[]{:S(2)}) async-start(), calls=%async_computation.1 | async-start | bytes 2228224 | tf_op jit(solution)/shard_map/all_gather | solution.py:24
  7.3 116.9 %all-gather.4.cloned.1.call-start = ((), (), s32[]{:S(2)}) async-start(), calls=%async_computation | async-start | bytes 4456448 | tf_op jit(solution)/shard_map/all_gather | solution.py:44
  9.6 4.2 %collective-permute-start = (bf16[1,896,32]{1,2,0:T(8,128)(2,1)S(1)}, bf16[1,896,32]{1,2,0:T(8,128)(2,1)S(1)}, u32[]{:S(2)}, u32[]{:S(2)}) collective-permute-start(bf16[1,896,32]{1,2,0:T(8,128)(2,1)S(1)} %get-tuple-element.18), channel_id=1, source_target_pairs={{0,1},{1,0},{2,3},{3,2},{4,5},{5,4},{6,7},{7,6},{8,9},{9,8},{10,11... | collective-permute-start | bytes 172040 | tf_op jit(solution)/shard_map/ppermute | solution.py:18
  10.3 5.8 %collective-permute-start.1 = (bf16[1,896,32]{1,2,0:T(8,128)(2,1)S(1)}, bf16[1,896,32]{1,2,0:T(8,128)(2,1)S(1)}, u32[]{:S(2)}, u32[]{:S(2)}) collective-permute-start(bf16[1,896,32]{1,2,0:T(8,128)(2,1)S(1)} %get-tuple-element.17), channel_id=1, source_target_pairs={{0,2},{1,3},{2,0},{3,1},{4,6},{5,7},{6,4},{7,5},{8,10},{9,11},{10,... | collective-permute-start | bytes 172040 | tf_op jit(solution)/shard_map/ppermute | solution.py:18
  11.6 5.7 %collective-permute-start.2 = (bf16[1,896,32]{1,2,0:T(8,128)(2,1)S(1)}, bf16[1,896,32]{1,2,0:T(8,128)(2,1)S(1)}, u32[]{:S(2)}, u32[]{:S(2)}) collective-permute-start(bf16[1,896,32]{1,2,0:T(8,128)(2,1)S(1)} %get-tuple-element.16), channel_id=1, source_target_pairs={{0,3},{1,2},{2,1},{3,0},{4,7},{5,6},{6,5},{7,4},{8,11},{9,10},{10,... | collective-permute-start | bytes 172040 | tf_op jit(solution)/shard_map/ppermute | solution.py:18
  12.0 5.4 %collective-permute-start.3 = (bf16[1,896,32]{1,2,0:T(8,128)(2,1)S(1)}, bf16[1,896,32]{1,2,0:T(8,128)(2,1)S(1)}, u32[]{:S(2)}, u32[]{:S(2)}) collective-permute-start(bf16[1,896,32]{1,2,0:T(8,128)(2,1)S(1)} %get-tuple-element.15), channel_id=1, source_target_pairs={{0,4},{1,5},{2,6},{3,7},{4,0},{5,1},{6,2},{7,3},{8,12},{9,13},{10,... | collective-permute-start | bytes 172040 | tf_op jit(solution)/shard_map/ppermute | solution.py:18
  13.3 6.1 %collective-permute-start.4 = (bf16[1,896,32]{1,2,0:T(8,128)(2,1)S(1)}, bf16[1,896,32]{1,2,0:T(8,128)(2,1)S(1)}, u32[]{:S(2)}, u32[]{:S(2)}) collective-permute-start(bf16[1,896,32]{1,2,0:T(8,128)(2,1)S(1)} %get-tuple-element.14), channel_id=1, source_target_pairs={{0,5},{1,4},{2,7},{3,6},{4,1},{5,0},{6,3},{7,2},{8,13},{9,12},{10,... | collective-permute-start | bytes 172040 | tf_op jit(solution)/shard_map/ppermute | solution.py:18
  13.8 6.7 %collective-permute-start.5 = (bf16[1,896,32]{1,2,0:T(8,128)(2,1)S(1)}, bf16[1,896,32]{1,2,0:T(8,128)(2,1)S(1)}, u32[]{:S(2)}, u32[]{:S(2)}) collective-permute-start(bf16[1,896,32]{1,2,0:T(8,128)(2,1)S(1)} %get-tuple-element.13), channel_id=1, source_target_pairs={{0,6},{1,7},{2,4},{3,5},{4,2},{5,3},{6,0},{7,1},{8,14},{9,15},{10,... | collective-permute-start | bytes 172040 | tf_op jit(solution)/shard_map/ppermute | solution.py:18
  16.1 7.7 %collective-permute-start.6 = (bf16[1,896,32]{1,2,0:T(8,128)(2,1)S(1)}, bf16[1,896,32]{1,2,0:T(8,128)(2,1)S(1)}, u32[]{:S(2)}, u32[]{:S(2)}) collective-permute-start(bf16[1,896,32]{1,2,0:T(8,128)(2,1)S(1)} %get-tuple-element.12), channel_id=1, source_target_pairs={{0,7},{1,6},{2,5},{3,4},{4,3},{5,2},{6,1},{7,0},{8,15},{9,14},{10,... | collective-permute-start | bytes 172040 | tf_op jit(solution)/shard_map/ppermute | solution.py:18
  17.3 6.6 %collective-permute-start.7 = (bf16[1,896,32]{1,2,0:T(8,128)(2,1)S(1)}, bf16[1,896,32]{1,2,0:T(8,128)(2,1)S(1)}, u32[]{:S(2)}, u32[]{:S(2)}) collective-permute-start(bf16[1,896,32]{1,2,0:T(8,128)(2,1)S(1)} %get-tuple-element.11), channel_id=1, source_target_pairs={{0,8},{1,9},{2,10},{3,11},{4,12},{5,13},{6,14},{7,15},{8,0},{9,1},... | collective-permute-start | bytes 172040 | tf_op jit(solution)/shard_map/ppermute | solution.py:18
  17.4 12.4 %collective-permute-start.8 = (bf16[1,896,32]{1,2,0:T(8,128)(2,1)S(1)}, bf16[1,896,32]{1,2,0:T(8,128)(2,1)S(1)}, u32[]{:S(2)}, u32[]{:S(2)}) collective-permute-start(bf16[1,896,32]{1,2,0:T(8,128)(2,1)S(1)} %get-tuple-element.10), channel_id=1, source_target_pairs={{0,9},{1,8},{2,11},{3,10},{4,13},{5,12},{6,15},{7,14},{8,1},{9,0},... | collective-permute-start | bytes 172040 | tf_op jit(solution)/shard_map/ppermute | solution.py:18
  19.4 12.6 %collective-permute-start.9 = (bf16[1,896,32]{1,2,0:T(8,128)(2,1)S(1)}, bf16[1,896,32]{1,2,0:T(8,128)(2,1)S(1)}, u32[]{:S(2)}, u32[]{:S(2)}) collective-permute-start(bf16[1,896,32]{1,2,0:T(8,128)(2,1)S(1)} %get-tuple-element.9), channel_id=1, source_target_pairs={{0,10},{1,11},{2,8},{3,9},{4,14},{5,15},{6,12},{7,13},{8,2},{9,3},... | collective-permute-start | bytes 172040 | tf_op jit(solution)/shard_map/ppermute | solution.py:18
  20.5 13.8 %collective-permute-start.10 = (bf16[1,896,32]{1,2,0:T(8,128)(2,1)S(1)}, bf16[1,896,32]{1,2,0:T(8,128)(2,1)S(1)}, u32[]{:S(2)}, u32[]{:S(2)}) collective-permute-start(bf16[1,896,32]{1,2,0:T(8,128)(2,1)S(1)} %get-tuple-element.8), channel_id=1, source_target_pairs={{0,11},{1,10},{2,9},{3,8},{4,15},{5,14},{6,13},{7,12},{8,3},{9,2},... | collective-permute-start | bytes 172040 | tf_op jit(solution)/shard_map/ppermute | solution.py:18
  23.8 15.3 %collective-permute-start.11 = (bf16[1,896,32]{1,2,0:T(8,128)(2,1)S(1)}, bf16[1,896,32]{1,2,0:T(8,128)(2,1)S(1)}, u32[]{:S(2)}, u32[]{:S(2)}) collective-permute-start(bf16[1,896,32]{1,2,0:T(8,128)(2,1)S(1)} %get-tuple-element.7), channel_id=1, source_target_pairs={{0,12},{1,13},{2,14},{3,15},{4,8},{5,9},{6,10},{7,11},{8,4},{9,5},... | collective-permute-start | bytes 172040 | tf_op jit(solution)/shard_map/ppermute | solution.py:18
  23.9 17.7 %collective-permute-start.12 = (bf16[1,896,32]{1,2,0:T(8,128)(2,1)S(1)}, bf16[1,896,32]{1,2,0:T(8,128)(2,1)S(1)}, u32[]{:S(2)}, u32[]{:S(2)}) collective-permute-start(bf16[1,896,32]{1,2,0:T(8,128)(2,1)S(1)} %get-tuple-element.6), channel_id=1, source_target_pairs={{0,13},{1,12},{2,15},{3,14},{4,9},{5,8},{6,11},{7,10},{8,5},{9,4},... | collective-permute-start | bytes 172040 | tf_op jit(solution)/shard_map/ppermute | solution.py:18
  29.9 13.9 %collective-permute-start.13 = (bf16[1,896,32]{1,2,0:T(8,128)(2,1)S(1)}, bf16[1,896,32]{1,2,0:T(8,128)(2,1)S(1)}, u32[]{:S(2)}, u32[]{:S(2)}) collective-permute-start(bf16[1,896,32]{1,2,0:T(8,128)(2,1)S(1)} %get-tuple-element.20), channel_id=1, source_target_pairs={{0,14},{1,15},{2,12},{3,13},{4,10},{5,11},{6,8},{7,9},{8,6},{9,7},... | collective-permute-start | bytes 172040 | tf_op jit(solution)/shard_map/ppermute | solution.py:18
  32.0 13.0 %collective-permute-start.14 = (bf16[1,896,32]{1,2,0:T(8,128)(2,1)S(1)}, bf16[1,896,32]{1,2,0:T(8,128)(2,1)S(1)}, u32[]{:S(2)}, u32[]{:S(2)}) collective-permute-start(bf16[1,896,32]{1,2,0:T(8,128)(2,1)S(1)} %get-tuple-element.5), channel_id=1, source_target_pairs={{0,15},{1,14},{2,13},{3,12},{4,11},{5,10},{6,9},{7,8},{8,7},{9,6},... | collective-permute-start | bytes 172040 | tf_op jit(solution)/shard_map/ppermute | solution.py:18
  67.1 53.6 %copy-start.1 = (u32[32]{0:T(128)S(1)}, u32[32]{0:T(128)}, u32[]{:S(2)}) copy-start(u32[32]{0:T(128)} %constant.55) | copy-start | bytes 388
  103.0 20.4 %collective-permute-start.17 = (f32[16,512]{1,0:T(8,128)S(1)}, f32[16,512]{1,0:T(8,128)S(1)}, u32[]{:S(2)}, u32[]{:S(2)}) collective-permute-start(f32[16,512]{1,0:T(8,128)S(1)} %fusion), channel_id=1, source_target_pairs={{0,3},{1,4},{2,5},{3,6},{4,7},{5,8},{6,9},{7,10},{8,11},{9,12},{10... | collective-permute-start | bytes 98312
  107.8 15.7 %collective-permute-start.16 = (f32[16,512]{1,0:T(8,128)S(1)}, f32[16,512]{1,0:T(8,128)S(1)}, u32[]{:S(2)}, u32[]{:S(2)}) collective-permute-start(f32[16,512]{1,0:T(8,128)S(1)} %fusion), channel_id=1, source_target_pairs={{0,2},{1,3},{2,4},{3,5},{4,6},{5,7},{6,8},{7,9},{8,10},{9,11},{10,... | collective-permute-start | bytes 98312
  113.0 10.5 %collective-permute-start.15 = (f32[16,512]{1,0:T(8,128)S(1)}, f32[16,512]{1,0:T(8,128)S(1)}, u32[]{:S(2)}, u32[]{:S(2)}) collective-permute-start(f32[16,512]{1,0:T(8,128)S(1)} %fusion), channel_id=1, source_target_pairs={{0,1},{1,2},{2,3},{3,4},{4,5},{5,6},{6,7},{7,8},{8,9},{9,10},{10,1... | collective-permute-start | bytes 98312
  118.8 4.7 %collective-permute-start.18 = (f32[12,512]{1,0:T(8,128)S(1)}, f32[12,512]{1,0:T(8,128)S(1)}, u32[]{:S(2)}, u32[]{:S(2)}) collective-permute-start(f32[12,512]{1,0:T(8,128)S(1)} %slice), channel_id=1, source_target_pairs={{0,4},{1,5},{2,6},{3,7},{4,8},{5,9},{6,10},{7,11},{8,12},{9,13},{1... | collective-permute-start | bytes 73736
Sparse Core Ops, SparseCore 0:
  9.5 50.1 all-gather.5
  61.9 52.9 all-gather.3
